TPU v7x, 32 devices: a whole 2x2x4 slice. The times are simulated.
32 devices in a mesh: row: 8 (over y, x, core), col: 4 (over z).
Axes of the slice: x: 2, y: 2, z: 4, core: 2. Of those that a mesh axis runs over, the one named last changes fastest.
Arguments:
- features: bfloat16 [16384, 1024], P(('row', 'col')), may hold values from 0 to 4, as said below
- coords: float32 [64, 16384], P(None, ('row', 'col')), may hold values from -1 to 1
Outputs:
- placed: float32 [64, 16384], P(None, ('row', 'col'))
- row_stress: float32 [16384], P(('row', 'col'))
- stress_norm: float32 [], replicated
Inputs may be any that keep to these rules, and one draw needn't show every extreme that they name: `features`: every molecule has at least one nonzero feature.
All inputs are finite; a program needn't handle non-finite values.
Results may differ from a plain program's by a relative error of at most 0.0003.
Values may be sent and summed in bfloat16 or wider, within the bound.
A program may use at most 192 MiB of HBM per device.

v0:
```python
import jax
import jax.numpy as jnp
from jax import lax
from jax.sharding import PartitionSpec as P

ITERS = 2


FLOOR = 0.25
EXACT = lax.Precision.HIGHEST


def from_root(block, axis, owner):
    block = jnp.where(lax.axis_index(axis) == owner, block, jnp.zeros_like(block))
    return lax.psum(block, axis)


def squares_of(values):
    return jnp.einsum("rf,rf->r", values, values, preferred_element_type=jnp.float32)


def tanimoto(left_rows, left_sq, right_rows):
    right_sq = squares_of(right_rows)
    common = lax.dot_general(
        left_rows, right_rows, (((1,), (1,)), ((), ())), preferred_element_type=jnp.float32
    )
    return 1.0 - common / (left_sq[:, None] + right_sq[None, :] - common)


def guttman_terms(dissim, x_rows, x_cols):
    coord_dim, row_len = x_rows.shape
    block_len = min(512, row_len)
    block_count = row_len // block_len
    col_norms = jnp.sum(x_cols * x_cols, axis=0)
    dis_blocks = dissim.reshape(block_count, block_len, dissim.shape[1])
    x_blocks = jnp.moveaxis(x_rows.reshape(coord_dim, block_count, block_len), 1, 0)

    def one_block(inputs):
        dis_blk, x_blk = inputs
        blk_norms = jnp.sum(x_blk * x_blk, axis=0)
        inner = lax.dot_general(
            x_blk,
            x_cols,
            (((0,), (0,)), ((), ())),
            precision=EXACT,
            preferred_element_type=jnp.float32,
        )
        distance = jnp.sqrt(
            jnp.maximum(blk_norms[:, None] + col_norms[None, :] - 2.0 * inner, FLOOR * FLOOR)
        )
        ratios = dis_blk / distance
        pulled = lax.dot_general(
            x_cols,
            ratios,
            (((1,), (1,)), ((), ())),
            precision=EXACT,
            preferred_element_type=jnp.float32,
        )
        pull_terms = x_blk * jnp.sum(ratios, axis=1)[None, :] - pulled
        stress = jnp.sum(jnp.square(dis_blk - distance), axis=1)
        return (pull_terms, stress)

    pull_terms, stress = lax.map(one_block, (dis_blocks, x_blocks))
    return (jnp.moveaxis(pull_terms, 0, 1).reshape(coord_dim, row_len), stress.reshape(row_len))


def on_device(features, coords):
    rows_n = lax.axis_size("row")
    cols_n = lax.axis_size("col")
    row_at = lax.axis_index("row")
    col_at = lax.axis_index("col")
    ratio_k = rows_n // cols_n
    share_len = coords.shape[1]
    row_len = share_len * cols_n
    molecules = row_len * rows_n
    feature_rows = lax.all_gather(features, "col", axis=0, tiled=True)
    rows_sq = squares_of(feature_rows)
    pieces = []
    for offset in range(ratio_k):
        feature_cols = from_root(feature_rows, "row", col_at * ratio_k + offset)
        pieces.append(tanimoto(feature_rows, rows_sq, feature_cols))
    dissim = jnp.concatenate(pieces, axis=1)
    dissim_sq = jnp.sum(dissim * dissim)
    current = coords
    row_stress = jnp.zeros((share_len,), jnp.float32)
    for sweep in range(ITERS):
        everything = lax.all_gather(current, ("row", "col"), axis=1, tiled=True)
        x_rows = lax.dynamic_slice_in_dim(everything, row_at * row_len, row_len, 1)
        x_cols = lax.dynamic_slice_in_dim(
            everything, col_at * row_len * ratio_k, row_len * ratio_k, 1
        )
        pull_terms, stress = guttman_terms(dissim, x_rows, x_cols)
        new_share, stress_share = (
            lax.psum_scatter(pull_terms, "col", scatter_dimension=1, tiled=True),
            lax.psum_scatter(stress, "col", scatter_dimension=0, tiled=True),
        )
        current = new_share / molecules
        row_stress = stress_share / molecules
    local_stress = jnp.sum(row_stress)
    stress_total, dissim_total = lax.psum((local_stress, dissim_sq), ("row", "col"))
    stress_norm = molecules * stress_total / dissim_total
    return (current, row_stress, stress_norm)


def solution(mesh):
    return jax.shard_map(
        on_device,
        mesh=mesh,
        in_specs=(P(("row", "col"), None), P(None, ("row", "col"))),
        out_specs=(P(None, ("row", "col")), P(("row", "col")), P()),
        check_vma=False,
    )
```

profile of v0, /device:TPU:8, one launch (start us, length us, event | category | flops | bytes accessed | tf_op | source)
XLA Modules:
  0.0 696.9 jit_solution(13126097829784607838)
XLA Ops:
  7.2 0.7 all-gather.6.cloned.1.call-update
  7.9 0.0 all-gather.4.cloned.1.call-start
  7.9 0.7 all-gather.4.cloned.1.call-update
  8.6 0.0 all-reduce.5.cloned.1.call-start
  8.7 80.2 %all-gather.6.cloned.1.call-done = bf16[2048,1024]{1,0:T(8,128)(2,1)} async-done(((bf16[512,1024]{1,0:T(8,128)(2,1)}), bf16[2048,1024]{1,0:T(8,128)(2,1)}) %all-gather.6.cloned.1.call-update) | async-done | bytes 4194320 | tf_op jit(solution)/shard_map/all_gather | solution.py:76
  88.9 6.0 broadcast_select_fusion.1
  94.9 0.0 reduce-scatter.3.cloned.1.call-start
  94.9 3.1 fusion.13
  98.0 57.0 %all-gather.4.cloned.1.call-done = f32[64,16384]{1,0:T(8,128)} async-done(((f32[64,512]{1,0:T(8,128)}), f32[64,16384]{1,0:T(8,128)}) %all-gather.4.cloned.1.call-update) | async-done | bytes 4194320 | tf_op jit(solution)/shard_map/all_gather | solution.py:87
  155.0 1.1 constant_dynamic-slice_fusion.5
  156.1 0.4 reshape.34
  156.4 1.4 multiply_reduce_fusion.4
  157.8 126.2 %all-reduce.5.cloned.1.call-done = (bf16[2048,1024]{1,0:T(8,128)(2,1)}, bf16[2048,1024]{1,0:T(8,128)(2,1)}) async-done(((bf16[2048,1024]{1,0:T(8,128)(2,1)}, bf16[2048,1024]{1,0:T(8,128)(2,1)}), (bf16[2048,1024]{1,0:T(8,128)(2,1)}, bf16[2048,1024]{1,0:T(8,128)(2,1)})) %all-reduce.5.cloned.1.call-update) | async-done | bytes 8388624 | tf_op jit(solution)/shard_map/psum | solution.py:15
  284.0 5.3 fusion.11
  289.3 11.4 %fusion.9 = f32[2048,2048]{0,1:T(8,128)S(1)} fusion(bf16[2048,1024]{1,0:T(8,128)(2,1)} %get-tuple-element.146, bf16[2048,1024]{1,0:T(8,128)(2,1)S(1)} %copy-done, f32[2048]{0:T(1024)S(1)} %get-tuple-element.161, f32[2048]{0:T(1024)S(1)} %fusion.13), kind=kOutput, calls=%fused_computation.25 | convolution fusion | flops 8606711808 | bytes 25182208 | tf_op jit(solution)/shard_map/dot_general | solution.py:24
  300.7 14.4 %fusion.10 = f32[2048,2048]{0,1:T(8,128)} fusion(bf16[2048,1024]{1,0:T(8,128)(2,1)} %get-tuple-element.145, bf16[2048,1024]{1,0:T(8,128)(2,1)S(1)} %copy-done, f32[2048]{0:T(1024)S(1)} %get-tuple-element.160, f32[2048]{0:T(1024)S(1)} %fusion.13), kind=kOutput, calls=%fused_computation.26 | convolution fusion | flops 8606711808 | bytes 25182208 | tf_op jit(solution)/shard_map/dot_general | solution.py:24
  315.2 20.2 %multiply_reduce_fusion.2 = (f32[]{:T(128)}, f32[2048,4096]{0,1:T(8,128)}) fusion(f32[2048,2048]{0,1:T(8,128)} %fusion.10, f32[2048,2048]{0,1:T(8,128)S(1)} %fusion.9), kind=kLoop, calls=%fused_computation.22 | loop fusion | flops 25165824 | bytes 67108864 | tf_op jit(solution)/shard_map/reduce_sum | solution.py:83
  335.4 31.1 %copy.33 = f32[2048,4096]{1,0:T(8,128)} copy(f32[2048,4096]{0,1:T(8,128)} %get-tuple-element.157) | data formatting | bytes 67108864 | tf_op jit(solution)/shard_map/while | solution.py:63
  366.5 78.5 %while.22 = (s32[]{:T(128)}, f32[4,64,512]{2,1,0:T(8,128)S(1)}, f32[4,64,512]{2,0,1:T(4,128)S(1)}, f32[4,512,4096]{2,1,0:T(8,128)}, f32[4096]{0:T(1024)S(1)}, /*index=5*/f32[64,4096]{1,0:T(8,128)S(1)}, s32[]{:T(128)}) while((s32[]{:T(128)}, f32[4,64,512]{2,1,0:T(8,128)S(1)}, f32[4,64,512]{2,0,1:T(4,128)S(1)}, f32[4,512,4096]{2,1,0:T(8,128)}, ...), condition=%wide.region_6.7_spmd, body=%wide.region_3.6_spmd.sunk | while | flops 3233938432 | bytes 28074072 | solution.py:63
  366.7 0.1 constant_dynamic-slice_fusion.10
  366.9 11.1 %fusion.37 = (f32[512]{0:T(512)S(1)}, f32[512,4096]{1,0:T(8,128)S(1)}) fusion(f32[64,4096]{1,0:T(8,128)S(1)} %get-tuple-element.271, f32[1,64,512]{2,0,1:T(1,128)S(1)} %constant_dynamic-slice_fusion.10, f32[4096]{0:T(1024)S(1)} %get-tuple-element.270, f32[512]{0:T(512)S(1)} %multiply_reduce_fusion.7, f32[4,512,4096]{2,1,0:T(8,128)} %get-tuple-element.269, ...), kind=kOutput, calls=%fused_computation.45.clone.1 | convolution fusion | flops 1623195136 | bytes 17977348 | tf_op jit(solution)/shard_map/while/body/eval_jaxpr/dot_general | solution.py:41
  378.0 8.2 %fusion.38 = f32[4,64,512]{2,1,0:T(8,128)S(1)} fusion(f32[4,64,512]{2,1,0:T(8,128)S(1)} %get-tuple-element.260, s32[]{:T(128)} %get-tuple-element.259, f32[512,4096]{1,0:T(8,128)S(1)} %get-tuple-element.240, f32[64,4096]{1,0:T(8,128)S(1)} %get-tuple-element.271, f32[1,64,512]{2,0,1:T(1,128)S(1)} %constant_dynamic-slice_fusion.10, ...), kind=kOutput, calls=%fused_computation.4.clone.1 | convolution fusion | flops 1610678272 | bytes 9701380 | tf_op jit(solution)/shard_map/while/body/eval_jaxpr/dot_general | solution.py:52
  386.3 0.1 constant_dynamic-slice_fusion.10
  386.5 11.1 %fusion.37 = (f32[512]{0:T(512)S(1)}, f32[512,4096]{1,0:T(8,128)S(1)}) fusion(f32[64,4096]{1,0:T(8,128)S(1)} %get-tuple-element.271, f32[1,64,512]{2,0,1:T(1,128)S(1)} %constant_dynamic-slice_fusion.10, f32[4096]{0:T(1024)S(1)} %get-tuple-element.270, f32[512]{0:T(512)S(1)} %multiply_reduce_fusion.7, f32[4,512,4096]{2,1,0:T(8,128)} %get-tuple-element.269, ...), kind=kOutput, calls=%fused_computation.45.clone.1 | convolution fusion | flops 1623195136 | bytes 17977348 | tf_op jit(solution)/shard_map/while/body/eval_jaxpr/dot_general | solution.py:41
  397.6 8.2 %fusion.38 = f32[4,64,512]{2,1,0:T(8,128)S(1)} fusion(f32[4,64,512]{2,1,0:T(8,128)S(1)} %get-tuple-element.260, s32[]{:T(128)} %get-tuple-element.259, f32[512,4096]{1,0:T(8,128)S(1)} %get-tuple-element.240, f32[64,4096]{1,0:T(8,128)S(1)} %get-tuple-element.271, f32[1,64,512]{2,0,1:T(1,128)S(1)} %constant_dynamic-slice_fusion.10, ...), kind=kOutput, calls=%fused_computation.4.clone.1 | convolution fusion | flops 1610678272 | bytes 9701380 | tf_op jit(solution)/shard_map/while/body/eval_jaxpr/dot_general | solution.py:52
  405.9 0.1 constant_dynamic-slice_fusion.10
  406.0 11.1 %fusion.37 = (f32[512]{0:T(512)S(1)}, f32[512,4096]{1,0:T(8,128)S(1)}) fusion(f32[64,4096]{1,0:T(8,128)S(1)} %get-tuple-element.271, f32[1,64,512]{2,0,1:T(1,128)S(1)} %constant_dynamic-slice_fusion.10, f32[4096]{0:T(1024)S(1)} %get-tuple-element.270, f32[512]{0:T(512)S(1)} %multiply_reduce_fusion.7, f32[4,512,4096]{2,1,0:T(8,128)} %get-tuple-element.269, ...), kind=kOutput, calls=%fused_computation.45.clone.1 | convolution fusion | flops 1623195136 | bytes 17977348 | tf_op jit(solution)/shard_map/while/body/eval_jaxpr/dot_general | solution.py:41
  417.2 8.2 %fusion.38 = f32[4,64,512]{2,1,0:T(8,128)S(1)} fusion(f32[4,64,512]{2,1,0:T(8,128)S(1)} %get-tuple-element.260, s32[]{:T(128)} %get-tuple-element.259, f32[512,4096]{1,0:T(8,128)S(1)} %get-tuple-element.240, f32[64,4096]{1,0:T(8,128)S(1)} %get-tuple-element.271, f32[1,64,512]{2,0,1:T(1,128)S(1)} %constant_dynamic-slice_fusion.10, ...), kind=kOutput, calls=%fused_computation.4.clone.1 | convolution fusion | flops 1610678272 | bytes 9701380 | tf_op jit(solution)/shard_map/while/body/eval_jaxpr/dot_general | solution.py:52
  425.4 0.1 constant_dynamic-slice_fusion.10
  425.6 11.1 %fusion.37 = (f32[512]{0:T(512)S(1)}, f32[512,4096]{1,0:T(8,128)S(1)}) fusion(f32[64,4096]{1,0:T(8,128)S(1)} %get-tuple-element.271, f32[1,64,512]{2,0,1:T(1,128)S(1)} %constant_dynamic-slice_fusion.10, f32[4096]{0:T(1024)S(1)} %get-tuple-element.270, f32[512]{0:T(512)S(1)} %multiply_reduce_fusion.7, f32[4,512,4096]{2,1,0:T(8,128)} %get-tuple-element.269, ...), kind=kOutput, calls=%fused_computation.45.clone.1 | convolution fusion | flops 1623195136 | bytes 17977348 | tf_op jit(solution)/shard_map/while/body/eval_jaxpr/dot_general | solution.py:41
  436.7 8.2 %fusion.38 = f32[4,64,512]{2,1,0:T(8,128)S(1)} fusion(f32[4,64,512]{2,1,0:T(8,128)S(1)} %get-tuple-element.260, s32[]{:T(128)} %get-tuple-element.259, f32[512,4096]{1,0:T(8,128)S(1)} %get-tuple-element.240, f32[64,4096]{1,0:T(8,128)S(1)} %get-tuple-element.271, f32[1,64,512]{2,0,1:T(1,128)S(1)} %constant_dynamic-slice_fusion.10, ...), kind=kOutput, calls=%fused_computation.4.clone.1 | convolution fusion | flops 1610678272 | bytes 9701380 | tf_op jit(solution)/shard_map/while/body/eval_jaxpr/dot_general | solution.py:52
  445.0 0.8 copy.36
  445.8 0.0 all-gather.8.cloned.1.call-start
  445.9 18.8 %reduce-scatter.3.cloned.1.call-done = f32[64,512]{1,0:T(8,128)} async-done(((f32[64,2048]{1,0:T(8,128)}), f32[64,512]{1,0:T(8,128)}) %reduce-scatter.3.cloned.1.call-update) | async-done | bytes 131088 | tf_op jit(solution)/shard_map/reduce_scatter | solution.py:94
  464.7 1.6 broadcast_multiply_fusion.1
  466.3 0.0 reduce-scatter.5.cloned.1.call-start
  466.4 65.6 %all-gather.8.cloned.1.call-done = f32[64,16384]{1,0:T(8,128)} async-done(((f32[64,512]{1,0:T(8,128)}), f32[64,16384]{1,0:T(8,128)}) %all-gather.8.cloned.1.call-update) | async-done | bytes 4194320 | tf_op jit(solution)/shard_map/all_gather | solution.py:87
  531.9 1.1 constant_dynamic-slice_fusion.3
  533.0 0.4 reshape.37
  533.4 1.4 multiply_reduce_fusion.3
  534.7 0.1 broadcast.36
  534.8 98.9 %while.23 = (s32[]{:T(128)}, f32[4,64,512]{2,1,0:T(8,128)S(1)}, f32[4,512]{1,0:T(4,128)S(1)}, f32[4,64,512]{2,0,1:T(4,128)S(1)}, f32[4,512,4096]{2,1,0:T(8,128)}...) while((s32[]{:T(128)}, f32[4,64,512]{2,1,0:T(8,128)S(1)}, ...), condition=%wide.region_13.14_spmd, body=%wide.region_9.13_spmd.sunk | while | flops 3242326528 | bytes 36469864 | solution.py:63
  535.1 0.1 constant_dynamic-slice_fusion.11
  535.2 13.9 %fusion.41 = (f32[512]{0:T(512)S(1)}, f32[512]{0:T(512)S(1)}, f32[512,4096]{1,0:T(8,128)S(1)}) fusion(f32[4,512,4096]{2,1,0:T(8,128)} %get-tuple-element.295, s32[]{:T(128)} %get-tuple-element.282, f32[64,4096]{1,0:T(8,128)S(1)} %get-tuple-element.297, f32[1,64,512]{2,0,1:T(1,128)S(1)} %constant_dynamic-slice_fusion.11, ...), kind=kOutput, calls=%fused_computation.11.clone.1 | convolution fusion | flops 1629486080 | bytes 17979396 | tf_op jit(solution)/shard_map/while/body/eval_jaxpr/dot_general | solution.py:41
  549.2 10.5 %fusion.42 = f32[4,64,512]{2,1,0:T(8,128)S(1)} fusion(f32[4,64,512]{2,1,0:T(8,128)S(1)} %get-tuple-element.283, s32[]{:T(128)} %get-tuple-element.282, f32[64,4096]{1,0:T(8,128)S(1)} %get-tuple-element.297, f32[1,64,512]{2,0,1:T(1,128)S(1)} %constant_dynamic-slice_fusion.11, f32[512]{0:T(512)S(1)} %get-tuple-element.249, ...), kind=kOutput, calls=%fused_computation.16.clone.1 | convolution fusion | flops 1612775424 | bytes 18091008 | tf_op jit(solution)/shard_map/while/body/eval_jaxpr/dot_general | solution.py:52
  559.7 0.1 dynamic_update_slice.18
  559.7 0.1 constant_dynamic-slice_fusion.11
  559.9 13.9 %fusion.41 = (f32[512]{0:T(512)S(1)}, f32[512]{0:T(512)S(1)}, f32[512,4096]{1,0:T(8,128)S(1)}) fusion(f32[4,512,4096]{2,1,0:T(8,128)} %get-tuple-element.295, s32[]{:T(128)} %get-tuple-element.282, f32[64,4096]{1,0:T(8,128)S(1)} %get-tuple-element.297, f32[1,64,512]{2,0,1:T(1,128)S(1)} %constant_dynamic-slice_fusion.11, ...), kind=kOutput, calls=%fused_computation.11.clone.1 | convolution fusion | flops 1629486080 | bytes 17979396 | tf_op jit(solution)/shard_map/while/body/eval_jaxpr/dot_general | solution.py:41
  573.8 10.5 %fusion.42 = f32[4,64,512]{2,1,0:T(8,128)S(1)} fusion(f32[4,64,512]{2,1,0:T(8,128)S(1)} %get-tuple-element.283, s32[]{:T(128)} %get-tuple-element.282, f32[64,4096]{1,0:T(8,128)S(1)} %get-tuple-element.297, f32[1,64,512]{2,0,1:T(1,128)S(1)} %constant_dynamic-slice_fusion.11, f32[512]{0:T(512)S(1)} %get-tuple-element.249, ...), kind=kOutput, calls=%fused_computation.16.clone.1 | convolution fusion | flops 1612775424 | bytes 18091008 | tf_op jit(solution)/shard_map/while/body/eval_jaxpr/dot_general | solution.py:52
  584.3 0.1 dynamic_update_slice.18
  584.4 0.1 constant_dynamic-slice_fusion.11
  584.5 13.9 %fusion.41 = (f32[512]{0:T(512)S(1)}, f32[512]{0:T(512)S(1)}, f32[512,4096]{1,0:T(8,128)S(1)}) fusion(f32[4,512,4096]{2,1,0:T(8,128)} %get-tuple-element.295, s32[]{:T(128)} %get-tuple-element.282, f32[64,4096]{1,0:T(8,128)S(1)} %get-tuple-element.297, f32[1,64,512]{2,0,1:T(1,128)S(1)} %constant_dynamic-slice_fusion.11, ...), kind=kOutput, calls=%fused_computation.11.clone.1 | convolution fusion | flops 1629486080 | bytes 17979396 | tf_op jit(solution)/shard_map/while/body/eval_jaxpr/dot_general | solution.py:41
  598.5 10.5 %fusion.42 = f32[4,64,512]{2,1,0:T(8,128)S(1)} fusion(f32[4,64,512]{2,1,0:T(8,128)S(1)} %get-tuple-element.283, s32[]{:T(128)} %get-tuple-element.282, f32[64,4096]{1,0:T(8,128)S(1)} %get-tuple-element.297, f32[1,64,512]{2,0,1:T(1,128)S(1)} %constant_dynamic-slice_fusion.11, f32[512]{0:T(512)S(1)} %get-tuple-element.249, ...), kind=kOutput, calls=%fused_computation.16.clone.1 | convolution fusion | flops 1612775424 | bytes 18091008 | tf_op jit(solution)/shard_map/while/body/eval_jaxpr/dot_general | solution.py:52
  609.0 0.1 dynamic_update_slice.18
  609.0 0.1 constant_dynamic-slice_fusion.11
  609.2 13.9 %fusion.41 = (f32[512]{0:T(512)S(1)}, f32[512]{0:T(512)S(1)}, f32[512,4096]{1,0:T(8,128)S(1)}) fusion(f32[4,512,4096]{2,1,0:T(8,128)} %get-tuple-element.295, s32[]{:T(128)} %get-tuple-element.282, f32[64,4096]{1,0:T(8,128)S(1)} %get-tuple-element.297, f32[1,64,512]{2,0,1:T(1,128)S(1)} %constant_dynamic-slice_fusion.11, ...), kind=kOutput, calls=%fused_computation.11.clone.1 | convolution fusion | flops 1629486080 | bytes 17979396 | tf_op jit(solution)/shard_map/while/body/eval_jaxpr/dot_general | solution.py:41
  623.1 10.5 %fusion.42 = f32[4,64,512]{2,1,0:T(8,128)S(1)} fusion(f32[4,64,512]{2,1,0:T(8,128)S(1)} %get-tuple-element.283, s32[]{:T(128)} %get-tuple-element.282, f32[64,4096]{1,0:T(8,128)S(1)} %get-tuple-element.297, f32[1,64,512]{2,0,1:T(1,128)S(1)} %constant_dynamic-slice_fusion.11, f32[512]{0:T(512)S(1)} %get-tuple-element.249, ...), kind=kOutput, calls=%fused_computation.16.clone.1 | convolution fusion | flops 1612775424 | bytes 18091008 | tf_op jit(solution)/shard_map/while/body/eval_jaxpr/dot_general | solution.py:52
  633.6 0.1 dynamic_update_slice.18
  633.7 0.8 copy.37
  634.6 0.6 dynamic-slice
  635.8 9.0 %all-reduce = f32[2048]{0:T(1024)S(1)} all-reduce(f32[2048]{0:T(1024)S(1)} %bitcast.124), channel_id=4, replica_groups=mesh['row'=8,'col'=4] {'col'}, use_global_device_ids=true, to_apply=%region_15.16.clone | all-reduce | flops 2048 | bytes 16384
  644.8 1.3 fusion.14
  646.1 39.9 %all-reduce.1 = (f32[]{:T(128)}, f32[]{:T(128)}) all-reduce(f32[]{:T(128)} %get-tuple-element.147, f32[]{:T(128)} %get-tuple-element.156), channel_id=1, replica_groups=mesh['row'=8,'col'=4] {'row','col'}, use_global_device_ids=true, to_apply=%region_17.18 | all-reduce | flops 2 | bytes 16 | tf_op jit(solution)/shard_map/psum | solution.py:100
  687.4 1.6 broadcast_multiply_fusion
  (21 shorter events, 0.4 us)
Async XLA Ops:
  7.2 81.7 %all-gather.6.cloned.1.call-start = ((), (), s32[]{:S(2)}) async-start(), calls=%async_computation.3 | async-start | bytes 5242880 | tf_op jit(solution)/shard_map/all_gather | solution.py:76
  7.9 147.1 %all-gather.4.cloned.1.call-start = ((), (), s32[]{:S(2)}) async-start(), calls=%async_computation.2 | async-start | bytes 4325376 | tf_op jit(solution)/shard_map/all_gather | solution.py:87
  8.6 275.3 %all-reduce.5.cloned.1.call-start = ((), (), s32[]{:S(2)}) async-start(), calls=%async_computation.7 | async-start | bytes 16777216 | tf_op jit(solution)/shard_map/psum | solution.py:15
  94.9 369.9 %reduce-scatter.3.cloned.1.call-start = ((), (), s32[]{:S(2)}) async-start(), calls=%async_computation.4 | async-start | bytes 655360 | tf_op jit(solution)/shard_map/reduce_scatter | solution.py:94
  284.0 5.3 copy-start
  445.8 86.1 %all-gather.8.cloned.1.call-start = ((), (), s32[]{:S(2)}) async-start(), calls=%async_computation.5 | async-start | bytes 4325376 | tf_op jit(solution)/shard_map/all_gather | solution.py:87
  466.3 221.0 %reduce-scatter.5.cloned.1.call-start = ((), (), s32[]{:S(2)}) async-start(), calls=%async_computation.6 | async-start | bytes 655360 | tf_op jit(solution)/shard_map/reduce_scatter | solution.py:94
  534.8 99.8 %copy-start.1 = (u32[32]{0:T(128)S(1)}, u32[32]{0:T(128)}, u32[]{:S(2)}) copy-start(u32[32]{0:T(128)} %constant.75) | copy-start | bytes 388
Sparse Core Ops, SparseCore 0:
  9.6 79.2 all-gather.5
  91.9 63.0 all-gather.3
  158.7 125.2 all-reduce.4
  446.0 18.7 reduce-scatter.2
  468.7 63.2 all-gather.7
  634.7 17.1 reduce-scatter.4
where the time goes:
time: 699 us; the launch traced here: 697 us
  waiting for transfers between devices  349 us (50%)
  matrix products  201 us (29%)
  blocking collectives  48.9 us (7%)
  other arithmetic  41.9 us (6%)
  local copies, waits for them, and re-layouts  37.5 us (5%)
  between operations  17.4 us (2%)
    psum x1, waiting for transfers between devices, from_root(): return lax.psum(block, axis)  126 us
    all_gather x2, waiting for transfers between devices, on_device(): everything = lax.all_gather(current, ('row', 'col'), axis=1, tiled=True)  123 us
    dot_general x8, matrix products, one_block(): lax.dot_general(x_blk, x_cols, (((0,), (0,)), ((), ())), precision=EXACT,...  100 us
    all_gather x1, waiting for transfers between devices, on_device(): feature_rows = lax.all_gather(features, 'col', axis=0, tiled=True)  80.2 us
    dot_general x8, matrix products, one_block(): lax.dot_general(x_cols, ratios, (((1,), (1,)), ((), ())), precision=EXACT...  74.9 us
    psum x1, blocking collectives, on_device(): lax.psum((local_stress, dissim_sq), ('row', 'col'))  39.9 us
    while x1, local copies, waits for them, and re-layouts, guttman_terms(): pull_terms, stress = lax.map(one_block, (dis_blocks, x_blocks))  31.1 us
    dot_general x2, matrix products, tanimoto(): lax.dot_general(left_rows, right_rows, (((1,), (1,)), ((), ())), preferre...  25.8 us
  transfers between devices with their start and end apart: 6, of which 5 were waited for; matrix products, arithmetic and copies ran while one was open for 2% of the time, Pallas kernels for 0%

commit v1 on v0

v1 whole, which is shorter than its diff:
```python
import functools

import jax
import jax.numpy as jnp
from jax import lax
from jax.experimental import pallas as pl
from jax.experimental.pallas import tpu as pltpu
from jax.sharding import PartitionSpec as P

ITERS = 2
FLOOR = 0.25
AUX = 72


def halves(x):
    high = lax.reduce_precision(x, 8, 7)
    low = lax.reduce_precision(x - high, 8, 7)
    return high, low


def operands(high, low, norms):
    dim, length = high.shape
    left = jnp.concatenate([-2.0 * high, -2.0 * high, -2.0 * low, -2.0 * low], axis=0).T
    right = jnp.concatenate([high, low, high, low], axis=0)
    ones = jnp.ones((dim, length), jnp.float32)
    weights = jnp.concatenate([high, low, ones, jnp.zeros_like(ones)], axis=0).T
    return left.astype(jnp.bfloat16), right.astype(jnp.bfloat16), weights.astype(jnp.bfloat16)


def guttman_chunk(dissim, left, right, weights, row_norm, col_norm):
    cross = jnp.dot(left, right, preferred_element_type=jnp.float32)
    dist_sq = jnp.maximum((row_norm + col_norm) + cross, FLOOR * FLOOR)
    inverse = lax.rsqrt(dist_sq)
    ratio = dissim * inverse
    high = ratio.astype(jnp.bfloat16)
    low = (ratio - high.astype(jnp.float32)).astype(jnp.bfloat16)
    moved = jnp.dot(high, weights, preferred_element_type=jnp.float32)
    moved += jnp.dot(low, weights, preferred_element_type=jnp.float32)
    return moved, dist_sq * inverse


def lanes_sum(values):
    total = values[:, :128]
    for at in range(128, values.shape[1], 128):
        total += values[:, at : at + 128]
    return total


def pull_of(moved, x_rows):
    dim = x_rows.shape[1]
    row_sum = moved[:, 2 * dim : 2 * dim + 1]
    return x_rows * row_sum - (moved[:, :dim] + moved[:, dim : 2 * dim])


def first_kernel(chunk, rows_ref, cols_ref, row_sq_ref, col_sq_ref, left_ref, right_ref, weights_ref,
                 row_norm_ref, col_norm_ref, x_ref, dissim_ref, pull_ref, square_ref):
    tile, cols_len = dissim_ref.shape
    rows = rows_ref[...]
    left = left_ref[...]
    row_sq = row_sq_ref[...]
    row_norm = row_norm_ref[...]
    moved = jnp.zeros((tile, weights_ref.shape[1]), jnp.float32)
    squares = jnp.zeros((tile, 128), jnp.float32)
    for start in range(0, cols_len, chunk):
        at = slice(start, start + chunk)
        common = lax.dot_general(
            rows, cols_ref[at, :], (((1,), (1,)), ((), ())), preferred_element_type=jnp.float32
        )
        dissim = 1.0 - common / ((row_sq + col_sq_ref[:, at]) - common)
        dissim_ref[:, at] = dissim
        squares += lanes_sum(dissim * dissim)
        part, _ = guttman_chunk(
            dissim, left, right_ref[:, at], weights_ref[at, :], row_norm, col_norm_ref[:, at]
        )
        moved += part
    pull_ref[...] = pull_of(moved, x_ref[...]).T
    square_ref[...] = jnp.sum(squares.reshape(tile // 8, 8, 128), axis=0)[None]


def later_kernel(chunk, dissim_ref, left_ref, right_ref, weights_ref, row_norm_ref, col_norm_ref, x_ref,
                 pull_ref):
    tile, cols_len = dissim_ref.shape
    dim = x_ref.shape[1]
    left = left_ref[...]
    row_norm = row_norm_ref[...]
    moved = jnp.zeros((tile, weights_ref.shape[1]), jnp.float32)
    misfit = jnp.zeros((tile, 128), jnp.float32)
    for start in range(0, cols_len, chunk):
        at = slice(start, start + chunk)
        dissim = dissim_ref[:, at]
        part, dist = guttman_chunk(
            dissim, left, right_ref[:, at], weights_ref[at, :], row_norm, col_norm_ref[:, at]
        )
        gap = dissim - dist
        misfit += lanes_sum(gap * gap)
        moved += part
    stress = jnp.sum(misfit, axis=1, keepdims=True)
    pull_ref[:dim, :] = pull_of(moved, x_ref[...]).T
    pull_ref[dim:, :] = jnp.broadcast_to(stress, (tile, 128)).T[: AUX - dim]


def on_device(features, coords):
    rows_n = lax.axis_size("row")
    cols_n = lax.axis_size("col")
    dim, share_len = coords.shape
    feat = features.shape[1]
    row_len = share_len * cols_n
    col_len = share_len * rows_n
    molecules = row_len * rows_n
    tile = 256
    chunk = 512
    steps = row_len // tile
    params = pltpu.CompilerParams(vmem_limit_bytes=56 * 1024 * 1024)

    by_row = lambda width: pl.BlockSpec((tile, width), lambda i: (i, 0))
    whole = lambda *shape: pl.BlockSpec(shape, lambda i: (0, 0))

    feature_rows = lax.all_gather(features, "col", axis=0, tiled=True)
    feature_cols = lax.all_gather(features, "row", axis=0, tiled=True)
    wide = features.astype(jnp.float32)
    share_sq = jnp.sum(wide * wide, axis=1)
    zeros = jnp.zeros((AUX - dim - 1, share_len), jnp.float32)

    def spread(current, extra):
        packed = jnp.concatenate([current, extra[None, :], zeros], axis=0)
        return (
            lax.all_gather(packed, "col", axis=1, tiled=True),
            lax.all_gather(packed, "row", axis=1, tiled=True),
        )

    def prepare(rows_aux, cols_aux):
        row_high, row_low = halves(rows_aux[:dim])
        col_high, col_low = halves(cols_aux[:dim])
        row_hat = row_high + row_low
        col_hat = col_high + col_low
        row_norm = jnp.sum(row_hat * row_hat, axis=0)[:, None]
        col_norm = jnp.sum(col_hat * col_hat, axis=0)[None, :]
        left, _, _ = operands(row_high, row_low, row_norm)
        _, right, weights = operands(col_high, col_low, col_norm)
        return left, right, weights, row_norm, col_norm, rows_aux[:dim].T

    guttman_specs = [
        by_row(4 * dim),
        whole(4 * dim, col_len),
        whole(col_len, 4 * dim),
        by_row(1),
        whole(1, col_len),
        by_row(dim),
    ]

    rows_aux, cols_aux = spread(coords, share_sq)
    dissim, pull, squares = pl.pallas_call(
        functools.partial(first_kernel, chunk),
        grid=(steps,),
        in_specs=[by_row(feat), whole(col_len, feat), by_row(1), whole(1, col_len)] + guttman_specs,
        out_specs=[
            by_row(col_len),
            pl.BlockSpec((dim, tile), lambda i: (0, i)),
            pl.BlockSpec((1, 8, 128), lambda i: (i, 0, 0)),
        ],
        out_shape=[
            jax.ShapeDtypeStruct((row_len, col_len), jnp.float32),
            jax.ShapeDtypeStruct((dim, row_len), jnp.float32),
            jax.ShapeDtypeStruct((steps, 8, 128), jnp.float32),
        ],
        compiler_params=params,
    )(
        feature_rows,
        feature_cols,
        rows_aux[dim][:, None],
        cols_aux[dim][None, :],
        *prepare(rows_aux, cols_aux),
    )
    dissim_sq = jnp.sum(squares)
    current = lax.psum_scatter(pull, "col", scatter_dimension=1, tiled=True) / molecules
    for sweep in range(1, ITERS):
        rows_aux = lax.all_gather(current, "col", axis=1, tiled=True)
        cols_aux = lax.all_gather(current, "row", axis=1, tiled=True)
        pull = pl.pallas_call(
            functools.partial(later_kernel, chunk),
            grid=(steps,),
            in_specs=[by_row(col_len)] + guttman_specs,
            out_specs=pl.BlockSpec((AUX, tile), lambda i: (0, i)),
            out_shape=jax.ShapeDtypeStruct((AUX, row_len), jnp.float32),
            compiler_params=params,
        )(dissim, *prepare(rows_aux, cols_aux))
        reduced = lax.psum_scatter(pull, "col", scatter_dimension=1, tiled=True) / molecules
        current = reduced[:dim]
        row_stress = reduced[dim]
    stress_total, dissim_total = lax.psum((jnp.sum(row_stress), dissim_sq), ("row", "col"))
    stress_norm = molecules * stress_total / dissim_total
    return (current, row_stress, stress_norm)


def solution(mesh):
    return jax.shard_map(
        on_device,
        mesh=mesh,
        in_specs=(P(("row", "col"), None), P(None, ("row", "col"))),
        out_specs=(P(None, ("row", "col")), P(("row", "col")), P()),
        check_vma=False,
    )
```

time: 699 us -> 398 us (0.57)
  matrix products: 201 us -> 0 us
  waiting for transfers between devices: 349 us -> 173 us
  Pallas kernels: 0 us -> 78.3 us
  blocking collectives: 48.9 us -> 85.4 us
  other arithmetic: 41.9 us -> 22 us
  local copies, waits for them, and re-layouts: 37.5 us -> 20.8 us
    dot_general x18 -> x0, matrix products: 201 us -> none  [the longest x8 100 us: one_block(): lax.dot_general(x_blk, x_cols, (((0,), (0,)), ((), ())), precision=EXACT,...]
    psum x1 -> x0, waiting for transfers between devices: 126 us -> none  [from_root(): return lax.psum(block, axis)]
    pallas_call x0 -> x2, Pallas kernels: none -> 78.3 us  [the longest x1 46 us: on_device(): pl.pallas_call(functools.partial(first_kernel, chunk), grid=(steps,), in_...]
    all_gather x2 -> x3, waiting for transfers between devices: 123 us -> 61.5 us  [the longest x1 57.5 us: on_device(): feature_cols = lax.all_gather(features, 'row', axis=0, tiled=True)]
    all_gather x0 -> x2, blocking collectives: none -> 43.2 us  [the longest x1 21.6 us: on_device(): rows_aux = lax.all_gather(current, 'col', axis=1, tiled=True)]
    while x1 -> x0, local copies, waits for them, and re-layouts: 31.1 us -> none  [guttman_terms(): pull_terms, stress = lax.map(one_block, (dis_blocks, x_blocks))]
    reduce_scatter x2, waiting for transfers between devices: 18.9 us -> 44 us  [on_device(): lax.psum_scatter(pull, 'col', scatter_dimension=1, tiled=True) / molecules]
    reduce_sum x12 -> x6, other arithmetic: 24.4 us -> 8.01 us  [the longest x2 4.25 us: prepare(): col_norm = jnp.sum(col_hat * col_hat, axis=0)[None, :]]
  transfers between devices with their start and end apart: 6 -> 6, of which waited for: 5 -> 6; matrix products, arithmetic and copies ran while one was open for 2% -> 6% of each run, Pallas kernels for 0% -> 0%
where the time goes in v1:
time: 398 us; the launch traced here: 396 us
  waiting for transfers between devices  173 us (43%)
  blocking collectives  85.4 us (21%)
  Pallas kernels  78.3 us (20%)
  other arithmetic  22 us (6%)
  local copies, waits for them, and re-layouts  20.8 us (5%)
  between operations  16.6 us (4%)
    all_gather x1, waiting for transfers between devices, on_device(): feature_rows = lax.all_gather(features, 'col', axis=0, tiled=True)  66 us
    all_gather x1, waiting for transfers between devices, on_device(): feature_cols = lax.all_gather(features, 'row', axis=0, tiled=True)  57.5 us
    pallas_call x1, Pallas kernels, on_device(): pl.pallas_call(functools.partial(first_kernel, chunk), grid=(steps,), in_...  46 us
    reduce_scatter x2, waiting for transfers between devices, on_device(): lax.psum_scatter(pull, 'col', scatter_dimension=1, tiled=True) / molecules  44 us
    psum x1, blocking collectives, on_device(): lax.psum((jnp.sum(row_stress), dissim_sq), ('row', 'col'))  42.1 us
    pallas_call x1, Pallas kernels, on_device(): pl.pallas_call(functools.partial(later_kernel, chunk), grid=(steps,), in_...  32.2 us
    all_gather x1, blocking collectives, on_device(): rows_aux = lax.all_gather(current, 'col', axis=1, tiled=True)  21.6 us
    all_gather x1, blocking collectives, spread(): lax.all_gather(packed, 'col', axis=1, tiled=True)  21.6 us
  transfers between devices with their start and end apart: 6, of which 6 were waited for; matrix products, arithmetic and copies ran while one was open for 6% of the time, Pallas kernels for 0%

profile of v1, /device:TPU:8, one launch (start us, length us, event | category | flops | bytes accessed | tf_op | source)
XLA Modules:
  0.0 396.2 jit_solution(9584153313157349892)
XLA Ops:
  7.2 0.0 all-gather.9.cloned.1.call-start
  7.2 1.5 multiply_reduce_fusion
  8.7 0.1 copy.11
  8.9 1.0 copy.10
  9.9 0.1 pad.26.clone
  10.0 0.8 maximum_maximum_fusion
  10.8 0.0 copy-start.2
  10.8 0.0 all-gather.9.cloned.1.call-update
  10.9 0.0 all-gather.5.cloned.1.call-start
  10.9 0.7 all-gather.5.cloned.1.call-update
  11.6 0.0 all-gather.7.cloned.1.call-start
  11.7 0.7 all-gather.7.cloned.1.call-update
  12.3 0.0 reduce-scatter.3.cloned.1.call-start
  12.4 0.1 pad.15.clone
  12.5 0.0 copy-done.2
  12.5 21.6 %all_gather.20 = f32[72,2048]{0,1:T(8,128)S(1)} all-gather(f32[72,512]{0,1:T(8,128)S(1)} %copy-done.2), channel_id=1, replica_groups=mesh['row'=8,'col'=4] {'col'}, dimensions={1}, use_global_device_ids=true | all-gather | bytes 737280 | tf_op jit(solution)/shard_map/all_gather | solution.py:127
  34.1 1.3 slice_bitcast_fusion.1
  35.4 1.4 copy.14.row_norm_ref
  36.8 1.7 maximum_bitcast_fusion.left_ref
  38.4 1.3 slice_bitcast_fusion.row_sq_ref
  39.7 0.3 all-gather.9.cloned.1.call-done
  40.1 3.5 slice.26
  43.6 0.0 copy-start.1
  43.6 3.0 copy.12.col_sq_ref
  46.5 0.0 copy-done.1
  46.5 1.3 fusion.3
  47.9 3.0 fusion.10
  50.8 2.9 copy.13.right_ref
  53.8 66.0 %all-gather.5.cloned.1.call-done.rows_ref = bf16[2048,1024]{1,0:T(8,128)(2,1)} async-done(((bf16[512,1024]{1,0:T(8,128)(2,1)}), bf16[2048,1024]{1,0:T(8,128)(2,1)}) %all-gather.5.cloned.1.call-update) | async-done | bytes 4194320 | tf_op jit(solution)/shard_map/all_gather | solution.py:118
  119.8 57.5 %all-gather.7.cloned.1.call-done.cols_ref = bf16[4096,1024]{1,0:T(8,128)(2,1)} async-done(((bf16[512,1024]{1,0:T(8,128)(2,1)}), bf16[4096,1024]{1,0:T(8,128)(2,1)}) %all-gather.7.cloned.1.call-update) | async-done | bytes 8388624 | tf_op jit(solution)/shard_map/all_gather | solution.py:119
  177.3 46.0 %shard_map.49 = (f32[2048,4096]{1,0:T(8,128)}, f32[64,2048]{1,0:T(8,128)}, f32[8,8,128]{2,1,0:T(8,128)}) custom-call(bf16[2048,1024]{1,0:T(8,128)(2,1)} %all-gather.5.cloned.1.call-done.rows_ref, bf16[4096,1024]{1,0:T(8,128)(2,1)} %all-gather.7.cloned.1.call-done.cols_ref, f32[2048,1]{1,0:T(8,128)} %slice_bitcast_fusion.row_sq_ref, ...), custom_call_target="tpu_custom_call" | custom-call | tf_op jit(solution)/shard_map/pallas_call | solution.py:152
  223.3 2.4 copy.15
  225.7 0.0 reduce-scatter.3.cloned.1.call-update
  225.7 0.0 all-gather.11.cloned.1.call-start
  225.7 25.2 %reduce-scatter.3.cloned.1.call-done = f32[64,512]{0,1:T(8,128)} async-done(((f32[64,2048]{0,1:T(8,128)}), f32[64,512]{0,1:T(8,128)}) %reduce-scatter.3.cloned.1.call-update) | async-done | bytes 131088 | tf_op jit(solution)/shard_map/reduce_scatter | solution.py:175
  250.9 1.7 broadcast_multiply_fusion
  252.6 0.0 all-gather.11.cloned.1.call-update
  252.6 0.0 reduce-scatter.5.cloned.1.call-start
  252.7 21.6 %all_gather.22 = f32[64,2048]{0,1:T(8,128)S(1)} all-gather(f32[64,512]{0,1:T(8,128)} %broadcast_multiply_fusion), channel_id=1, replica_groups=mesh['row'=8,'col'=4] {'col'}, dimensions={1}, use_global_device_ids=true | all-gather | bytes 655360 | tf_op jit(solution)/shard_map/all_gather | solution.py:177
  274.3 0.0 copy-start
  274.3 0.4 fusion.25
  274.8 1.3 copy.17.row_norm_ref
  276.1 1.6 maximum_bitcast_fusion.1.left_ref
  277.7 0.0 copy-done
  277.7 3.7 all-gather.11.cloned.1.call-done
  281.5 2.9 fusion.7
  284.4 3.0 fusion.13
  287.4 3.0 copy.16.right_ref
  290.3 0.0 copy-start.3
  290.3 32.2 %shard_map.50 = f32[72,2048]{1,0:T(8,128)} custom-call(f32[2048,4096]{1,0:T(8,128)} %get-tuple-element.6.dissim_ref, bf16[2048,256]{1,0:T(8,128)(2,1)} %maximum_bitcast_fusion.1.left_ref, bf16[256,4096]{1,0:T(8,128)(2,1)} %copy.16.right_ref, bf16[4096,256]{1,0:T(8,128)(2,1)} %get-tuple-element.14.weights_ref, f32[2048,1]{1,0:T(8,128)} %copy.17.row_norm_ref, ...), custom_call_target="tpu_custom_call" | custom-call | tf_op jit(solution)/shard_map/pallas_call | solution.py:179
  322.5 0.0 reduce-scatter.5.cloned.1.call-update
  322.6 0.0 copy-done.3
  322.6 0.6 reduce_sum.69
  323.2 18.8 %reduce-scatter.5.cloned.1.call-done = f32[72,512]{1,0:T(8,128)} async-done(((f32[72,2048]{1,0:T(8,128)}), f32[72,512]{1,0:T(8,128)}) %reduce-scatter.5.cloned.1.call-update) | async-done | bytes 147472 | tf_op jit(solution)/shard_map/reduce_scatter | solution.py:187
  342.0 0.9 broadcast_multiply_fusion.1
  342.9 1.2 slice_reduce_fusion
  344.1 0.7 slice.29
  344.7 42.1 %all-reduce = (f32[]{:T(128)}, f32[]{:T(128)}) all-reduce(f32[]{:T(128)} %get-tuple-element.28, f32[]{:T(128)} %reduce_sum.69), channel_id=1, replica_groups=mesh['row'=8,'col'=4] {'row','col'}, use_global_device_ids=true, to_apply=%region_8.0 | all-reduce | flops 2 | bytes 16 | tf_op jit(solution)/shard_map/psum | solution.py:190
  (4 shorter events, 0.0 us)
Async XLA Ops:
  7.2 32.9 %all-gather.9.cloned.1.call-start = ((), (), s32[]{:S(2)}) async-start(), calls=%async_computation.4 | async-start | bytes 2359296 | tf_op jit(solution)/shard_map/all_gather | solution.py:128
  10.8 1.7 copy-start.2
  10.9 108.9 %all-gather.5.cloned.1.call-start = ((), (), s32[]{:S(2)}) async-start(), calls=%async_computation.2 | async-start | bytes 5242880 | tf_op jit(solution)/shard_map/all_gather | solution.py:118
  11.6 165.7 %all-gather.7.cloned.1.call-start = ((), (), s32[]{:S(2)}) async-start(), calls=%async_computation.3 | async-start | bytes 9437184 | tf_op jit(solution)/shard_map/all_gather | solution.py:119
  12.3 238.6 %reduce-scatter.3.cloned.1.call-start = ((), (), s32[]{:S(2)}) async-start(), calls=%async_computation.5 | async-start | bytes 1310720 | tf_op jit(solution)/shard_map/reduce_scatter | solution.py:175
  43.6 3.0 copy-start.1
  225.7 55.8 %all-gather.11.cloned.1.call-start = ((), (), s32[]{:S(2)}) async-start(), calls=%async_computation.6 | async-start | bytes 2359296 | tf_op jit(solution)/shard_map/all_gather | solution.py:178
  252.6 89.4 %reduce-scatter.5.cloned.1.call-start = ((), (), s32[]{:S(2)}) async-start(), calls=%async_computation.7 | async-start | bytes 737280 | tf_op jit(solution)/shard_map/reduce_scatter | solution.py:187
  274.3 3.4 copy-start
  290.3 32.2 %copy-start.3 = (f32[8,8,128]{2,1,0:T(8,128)S(1)}, f32[8,8,128]{2,1,0:T(8,128)}, u32[]{:S(2)}) copy-start(f32[8,8,128]{2,1,0:T(8,128)} %get-tuple-element.8) | copy-start | bytes 98308
Sparse Core Ops, SparseCore 0:
  11.0 29.0 all-gather.8
  41.6 78.1 all-gather.4
  121.7 55.5 all-gather.6
  225.8 25.0 reduce-scatter.2
  252.8 28.6 all-gather.10
  322.7 19.2 reduce-scatter.4

commit v2 on v0

v2 whole, which is shorter than its diff:
```python
import functools

import jax
import jax.numpy as jnp
from jax import lax
from jax.experimental import pallas as pl
from jax.experimental.pallas import tpu as pltpu
from jax.sharding import PartitionSpec as P

ITERS = 2
FLOOR = 0.25
LANES = 128
MESH = pl.DeviceIdType.MESH


def halves(x):
    high = lax.reduce_precision(x, 8, 7)
    return high, lax.reduce_precision(x - high, 8, 7)


def lanes_sum(values):
    total = values[:, :LANES]
    for at in range(LANES, values.shape[1], LANES):
        total += values[:, at : at + LANES]
    return total


def rows_sum(values):
    return jnp.sum(values.reshape(values.shape[0] // 8, 8, LANES), axis=0)


def with_norms(x, extra):
    length, dim = x.shape
    high, low = halves(x)
    hat = high + low
    norm = jnp.sum(hat * hat, axis=1, keepdims=True)
    lane = lax.broadcasted_iota(jnp.int32, (length, LANES - dim), 1)
    tail = jnp.where(lane == 0, norm, jnp.where(lane == 1, extra, 0.0))
    return jnp.concatenate([x, tail], axis=1)


def peers():
    row, col = lax.axis_index("row"), lax.axis_index("col")
    rows_n, cols_n = lax.axis_size("row"), lax.axis_size("col")
    along_row = [(k, (lax.rem(row + k, rows_n), col)) for k in range(1, rows_n)]
    along_col = [(k, (row, lax.rem(col + k, cols_n))) for k in range(1, cols_n)]
    return row, col, along_row, along_col


def greet(along_row, along_col):
    barrier = pltpu.get_barrier_semaphore()
    for _, device in along_row + along_col:
        pl.semaphore_signal(barrier, inc=1, device_id=device, device_id_type=MESH)
    pl.semaphore_wait(barrier, len(along_row) + len(along_col))


def send(source, target, sems, k, device):
    copy = pltpu.make_async_remote_copy(
        src_ref=source, dst_ref=target, send_sem=sems.at[0, k], recv_sem=sems.at[1, k],
        device_id=device, device_id_type=MESH,
    )
    copy.start()
    return copy


def gather_kernel(features_ref, aux_ref, frows_ref, fcols_ref, arows_ref, acols_ref, own, fr, fc, ar, ac):
    row, col, along_row, along_col = peers()
    local = []
    for at, (src, dst, place) in enumerate((
        (features_ref, frows_ref, col), (features_ref, fcols_ref, row),
        (aux_ref, arows_ref, col), (aux_ref, acols_ref, row),
    )):
        local.append(pltpu.make_async_copy(src, dst.at[place], own.at[at]))
        local[-1].start()
    greet(along_row, along_col)
    copies = []
    for k, device in along_col:
        copies.append(send(features_ref, frows_ref.at[col], fr, k, device))
    for k, device in along_row:
        copies.append(send(features_ref, fcols_ref.at[row], fc, k, device))
    for k, device in along_col:
        copies.append(send(aux_ref, arows_ref.at[col], ar, k, device))
    for k, device in along_row:
        copies.append(send(aux_ref, acols_ref.at[row], ac, k, device))
    for copy in local + copies:
        copy.wait()


def reduce_shares(pull_ref, inbox, sems, col, along_col, molecules):
    copies = []
    for k, device in along_col:
        copies.append(send(pull_ref.at[device[1]], inbox.at[col], sems, k, device))
    inbox[col] = pull_ref[col]
    for copy in copies:
        copy.wait()
    total = inbox[0]
    for at in range(1, len(along_col) + 1):
        total += inbox[at]
    return total / molecules


def turn_kernel(molecules, dim, pull_ref, arows_ref, acols_ref, inbox, mine, rs, ar, ac):
    row, col, along_row, along_col = peers()
    greet(along_row, along_col)
    total = reduce_shares(pull_ref, inbox, rs, col, along_col, molecules)
    aux = with_norms(total[:, :dim], 0.0)
    mine[...] = aux
    copies = []
    for k, device in along_col:
        copies.append(send(mine, arows_ref.at[col], ar, k, device))
    for k, device in along_row:
        copies.append(send(mine, acols_ref.at[row], ac, k, device))
    arows_ref[col] = aux
    acols_ref[row] = aux
    for copy in copies:
        copy.wait()


def last_kernel(molecules, pull_ref, part_ref, share_ref, total_ref, inbox, rowbox, colbox, mine, rs, sr, sc):
    row, col, along_row, along_col = peers()
    greet(along_row, along_col)
    copies = []
    for k, device in along_row:
        copies.append(send(part_ref, rowbox.at[row], sr, k, device))
    rowbox[row] = part_ref[...]
    for copy in copies:
        copy.wait()
    total = rowbox[0]
    for at in range(1, len(along_row) + 1):
        total += rowbox[at]
    mine[...] = total
    copies = []
    for k, device in along_col:
        copies.append(send(mine, colbox.at[col], sc, k, device))
    colbox[col] = total
    share_ref[...] = reduce_shares(pull_ref, inbox, rs, col, along_col, molecules)
    for copy in copies:
        copy.wait()
    total = colbox[0]
    for at in range(1, len(along_col) + 1):
        total += colbox[at]
    total_ref[...] = total


def prepare(dim, aux_ref, right, weights, lines):
    length = aux_ref.shape[0]
    piece = min(512, length)

    @pl.when(pl.program_id(0) == 0)
    def _():
        for start in range(0, length, piece):
            at = slice(start, start + piece)
            values = aux_ref[at, :]
            high, low = halves(values[:, :dim])
            right[at, :] = jnp.concatenate([high, low, high, low], axis=1).astype(jnp.bfloat16)
            ones = jnp.ones((piece, dim), jnp.float32)
            weights[at, :] = jnp.concatenate([high, low, ones, 0.0 * ones], axis=1).astype(jnp.bfloat16)
            lines[:, at] = values.T[dim : dim + 8]


def tile_kernel(first, chunk, dim, *refs):
    if first:
        rows_ref, cols_ref, arow_ref, acol_ref, dissim_ref, pull_ref, square_ref, right, weights, lines = refs
        rows = rows_ref[...]
    else:
        dissim_ref, arow_ref, acol_ref, pull_ref, square_ref, right, weights, lines = refs
    prepare(dim, acol_ref, right, weights, lines)
    tile, cols_len = dissim_ref.shape
    x = arow_ref[:, :dim]
    high, low = halves(x)
    left = (-2.0 * jnp.concatenate([high, high, low, low], axis=1)).astype(jnp.bfloat16)
    row_norm = arow_ref[:, dim : dim + 1]
    row_sq = arow_ref[:, dim + 1 : dim + 2]
    moved = jnp.zeros((tile, 4 * dim), jnp.float32)
    squares = jnp.zeros((tile, LANES), jnp.float32)
    contract = (((1,), (1,)), ((), ()))
    for start in range(0, cols_len, chunk):
        at = slice(start, start + chunk)
        if first:
            common = lax.dot_general(rows, cols_ref[at, :], contract, preferred_element_type=jnp.float32)
            dissim = 1.0 - common / ((row_sq + lines[1:2, at]) - common)
            dissim_ref[:, at] = dissim
        else:
            dissim = dissim_ref[:, at]
        cross = lax.dot_general(left, right[at, :], contract, preferred_element_type=jnp.float32)
        dist_sq = jnp.maximum((row_norm + lines[0:1, at]) + cross, FLOOR * FLOOR)
        inverse = lax.rsqrt(dist_sq)
        ratio = dissim * inverse
        gap = dissim if first else dissim - dist_sq * inverse
        squares += lanes_sum(gap * gap)
        top = ratio.astype(jnp.bfloat16)
        rest = (ratio - top.astype(jnp.float32)).astype(jnp.bfloat16)
        moved += jnp.dot(top, weights[at, :], preferred_element_type=jnp.float32)
        moved += jnp.dot(rest, weights[at, :], preferred_element_type=jnp.float32)
    pull = x * moved[:, 2 * dim : 2 * dim + 1] - (moved[:, :dim] + moved[:, dim : 2 * dim])
    stress = jnp.sum(squares, axis=1, keepdims=True)
    pull_ref[...] = jnp.concatenate([pull, jnp.broadcast_to(stress, (tile, LANES - dim))], axis=1)
    square_ref[...] = rows_sum(squares)[None]


def on_device(features, coords):
    rows_n = lax.axis_size("row")
    cols_n = lax.axis_size("col")
    dim, share_len = coords.shape
    feat = features.shape[1]
    row_len = share_len * cols_n
    col_len = share_len * rows_n
    molecules = row_len * rows_n
    tile = 256
    chunk = 512
    steps = row_len // tile
    big = 56 * 1024 * 1024
    f32 = jnp.float32
    any_spec = pl.BlockSpec(memory_space=pl.ANY)
    vmem = pl.BlockSpec(memory_space=pltpu.VMEM)
    dma = pltpu.SemaphoreType.DMA

    def shape(*sizes, dtype=f32):
        return jax.ShapeDtypeStruct(sizes, dtype)

    def comm(number):
        return pltpu.CompilerParams(collective_id=number, has_side_effects=True, vmem_limit_bytes=big)

    wide = features.astype(f32)
    aux = with_norms(coords.T, jnp.sum(wide * wide, axis=1, keepdims=True))
    frows, fcols, arows, acols = pl.pallas_call(
        gather_kernel,
        in_specs=[any_spec, any_spec],
        out_specs=[any_spec] * 4,
        out_shape=[
            shape(cols_n, share_len, feat, dtype=features.dtype),
            shape(rows_n, share_len, feat, dtype=features.dtype),
            shape(cols_n, share_len, LANES),
            shape(rows_n, share_len, LANES),
        ],
        scratch_shapes=[dma((4,)), dma((2, cols_n)), dma((2, rows_n)), dma((2, cols_n)), dma((2, rows_n))],
        compiler_params=comm(0),
    )(features, aux)

    by_row = lambda width: pl.BlockSpec((tile, width), lambda i: (i, 0))
    whole = lambda *sizes: pl.BlockSpec(sizes, lambda i: (0, 0))

    def tiles(first, *given):
        specs = [by_row(feat), whole(col_len, feat)] if first else [by_row(col_len)]
        outs = [by_row(LANES), pl.BlockSpec((1, 8, LANES), lambda i: (i, 0, 0))]
        shapes = [shape(row_len, LANES), shape(steps, 8, LANES)]
        if first:
            outs, shapes = [by_row(col_len)] + outs, [shape(row_len, col_len)] + shapes
        return pl.pallas_call(
            functools.partial(tile_kernel, first, chunk, dim),
            grid=(steps,),
            in_specs=specs + [by_row(LANES), whole(col_len, LANES)],
            out_specs=outs,
            out_shape=shapes,
            scratch_shapes=[
                pltpu.VMEM((col_len, 4 * dim), jnp.bfloat16),
                pltpu.VMEM((col_len, 4 * dim), jnp.bfloat16),
                pltpu.VMEM((8, col_len), f32),
            ],
            compiler_params=pltpu.CompilerParams(vmem_limit_bytes=big),
        )(*given)

    dissim, pull, dis_squares = tiles(
        True, frows.reshape(row_len, feat), fcols.reshape(col_len, feat),
        arows.reshape(row_len, LANES), acols.reshape(col_len, LANES),
    )
    inbox = pltpu.VMEM((cols_n, share_len, LANES), f32)
    mine = pltpu.VMEM((share_len, LANES), f32)
    for sweep in range(1, ITERS):
        arows, acols = pl.pallas_call(
            functools.partial(turn_kernel, molecules, dim),
            in_specs=[vmem],
            out_specs=[vmem, vmem],
            out_shape=[shape(cols_n, share_len, LANES), shape(rows_n, share_len, LANES)],
            scratch_shapes=[inbox, mine, dma((2, cols_n)), dma((2, cols_n)), dma((2, rows_n))],
            compiler_params=comm(sweep),
        )(pull.reshape(cols_n, share_len, LANES))
        pull, misfits = tiles(False, dissim, arows.reshape(row_len, LANES), acols.reshape(col_len, LANES))
    parts = jnp.stack([jnp.sum(misfits, axis=0), jnp.sum(dis_squares, axis=0)])
    share, totals = pl.pallas_call(
        functools.partial(last_kernel, molecules),
        in_specs=[vmem, vmem],
        out_specs=[vmem, vmem],
        out_shape=[shape(share_len, LANES), shape(2, 8, LANES)],
        scratch_shapes=[
            inbox, pltpu.VMEM((rows_n, 2, 8, LANES), f32), pltpu.VMEM((cols_n, 2, 8, LANES), f32),
            pltpu.VMEM((2, 8, LANES), f32), dma((2, cols_n)), dma((2, rows_n)), dma((2, cols_n)),
        ],
        compiler_params=comm(ITERS),
    )(pull.reshape(cols_n, share_len, LANES), parts)
    totals = jnp.sum(totals, axis=(1, 2))
    return (share[:, :dim].T, share[:, dim], totals[0] / totals[1])


def solution(mesh):
    return jax.shard_map(
        on_device,
        mesh=mesh,
        in_specs=(P(("row", "col"), None), P(None, ("row", "col"))),
        out_specs=(P(None, ("row", "col")), P(("row", "col")), P()),
        check_vma=False,
    )
```

time: 699 us -> 296 us (0.42)
  waiting for transfers between devices: 349 us -> 0 us
  Pallas kernels: 0 us -> 282 us
  matrix products: 201 us -> 0 us
  blocking collectives: 48.9 us -> 0 us
  other arithmetic: 41.9 us -> 5.63 us
  local copies, waits for them, and re-layouts: 37.5 us -> 5.12 us
  between operations: 17.4 us -> 3.15 us
    pallas_call x0 -> x5, Pallas kernels: none -> 282 us  [the longest x1 118 us: on_device(): pl.pallas_call(gather_kernel, in_specs=[any_spec, any_spec], out_specs=[a...]
    all_gather x3 -> x0, waiting for transfers between devices: 203 us -> none  [the longest x2 123 us: on_device(): everything = lax.all_gather(current, ('row', 'col'), axis=1, tiled=True)]
    dot_general x18 -> x0, matrix products: 201 us -> none  [the longest x8 100 us: one_block(): lax.dot_general(x_blk, x_cols, (((0,), (0,)), ((), ())), precision=EXACT,...]
    psum x1 -> x0, waiting for transfers between devices: 126 us -> none  [from_root(): return lax.psum(block, axis)]
    psum x1 -> x0, blocking collectives: 39.9 us -> none  [on_device(): lax.psum((local_stress, dissim_sq), ('row', 'col'))]
    while x1 -> x0, local copies, waits for them, and re-layouts: 31.1 us -> none  [guttman_terms(): pull_terms, stress = lax.map(one_block, (dis_blocks, x_blocks))]
    reduce_sum x12 -> x5, other arithmetic: 24.4 us -> 3.99 us  [the longest x2 1.54 us: on_device(): parts = jnp.stack([jnp.sum(misfits, axis=0), jnp.sum(dis_squares, axis=0)])]
    reduce_scatter x2 -> x0, waiting for transfers between devices: 18.9 us -> none  [on_device(): lax.psum_scatter(pull_terms, 'col', scatter_dimension=1, tiled=True)]
  transfers between devices with their start and end apart: 6 -> 0, of which waited for: 5 -> 0; matrix products, arithmetic and copies ran while one was open for 2% -> 0% of each run, Pallas kernels for 0% -> 0%
where the time goes in v2:
time: 296 us
  Pallas kernels  282 us (95%)
  other arithmetic  5.63 us (2%)
  local copies, waits for them, and re-layouts  5.12 us (2%)
  between operations  3.15 us (1%)
    pallas_call x1, Pallas kernels, on_device(): pl.pallas_call(gather_kernel, in_specs=[any_spec, any_spec], out_specs=[a...  118 us
    pallas_call x2, Pallas kernels, tiles(): pl.pallas_call(functools.partial(tile_kernel, first, chunk, dim), grid=(s...  78.2 us
    pallas_call x1, Pallas kernels, on_device(): pl.pallas_call(functools.partial(turn_kernel, molecules, dim), in_specs=[...  52 us
    pallas_call x1, Pallas kernels, on_device(): pl.pallas_call(functools.partial(last_kernel, molecules), in_specs=[vmem,...  33.5 us

profile of v2, /device:TPU:8, one launch (start us, length us, event | category | flops | bytes accessed | tf_op | source)
XLA Modules:
  0.0 295.9 jit_solution(11663568300504873786)
XLA Ops:
  0.6 1.5 multiply_reduce_fusion
  2.1 1.0 copy.7
  3.2 0.2 fusion.2
  3.3 0.2 select_select_fusion
  3.5 0.8 pad_maximum_fusion.aux_ref
  4.4 118.3 %shard_map.49 = (bf16[4,512,1024]{2,1,0:T(8,128)(2,1)}, bf16[8,512,1024]{2,1,0:T(8,128)(2,1)}, f32[4,512,128]{2,1,0:T(8,128)}, f32[8,512,128]{2,1,0:T(8,128)}) custom-call(bf16[512,1024]{1,0:T(8,128)(2,1)} %features_ref.1, f32[512,128]{1,0:T(8,128)} %pad_maximum_fusion.aux_ref), custom_call_target="tpu_custom_call" | custom-call | tf_op jit(solution)/shard_map/pallas_call | solution.py:226
  122.7 46.4 %shard_map.50 = (f32[2048,4096]{1,0:T(8,128)}, f32[2048,128]{1,0:T(8,128)}, f32[8,8,128]{2,1,0:T(8,128)}) custom-call(bf16[2048,1024]{1,0:T(8,128)(2,1)} %bitcast.16, bf16[4096,1024]{1,0:T(8,128)(2,1)} %bitcast.15, f32[2048,128]{1,0:T(8,128)} %bitcast.23, f32[4096,128]{1,0:T(8,128)} %bitcast.18), custom_call_target="tpu_custom_call" | custom-call | tf_op jit(solution)/shard_map/pallas_call | solution.py:249
  169.1 0.8 reduce_sum.48
  169.8 52.0 %shard_map.51 = (f32[4,512,128]{2,1,0:T(8,128)}, f32[8,512,128]{2,1,0:T(8,128)}) custom-call(f32[4,512,128]{2,1,0:T(8,128)} %bitcast.22), custom_call_target="tpu_custom_call" | custom-call | tf_op jit(solution)/shard_map/pallas_call | solution.py:270
  221.8 31.8 %shard_map.52 = (f32[2048,128]{1,0:T(8,128)}, f32[8,8,128]{2,1,0:T(8,128)}) custom-call(f32[2048,4096]{1,0:T(8,128)} %get-tuple-element.20.refs_0_, f32[2048,128]{1,0:T(8,128)} %bitcast.20, f32[4096,128]{1,0:T(8,128)} %bitcast.19), custom_call_target="tpu_custom_call" | custom-call | tf_op jit(solution)/shard_map/pallas_call | solution.py:249
  253.6 0.8 reduce_sum.47
  254.4 0.6 pad_maximum_fusion.1.part_ref
  255.0 33.5 %shard_map.53 = (f32[512,128]{1,0:T(8,128)}, f32[2,8,128]{2,1,0:T(8,128)}) custom-call(f32[4,512,128]{2,1,0:T(8,128)} %bitcast.21, f32[2,8,128]{2,1,0:T(8,128)} %pad_maximum_fusion.1.part_ref), custom_call_target="tpu_custom_call" | custom-call | tf_op jit(solution)/shard_map/pallas_call | solution.py:280
  288.5 0.8 reduce_sum.49
  289.3 0.6 fusion.3
  291.3 1.8 slice_reduce_fusion
  293.0 1.0 slice_bitcast_fusion
  294.0 0.8 copy.8
  (1 shorter events, 0.0 us)

commit v3 on v2

--- a/solution.py
+++ b/solution.py
@@ -63,7 +63,82 @@
     return copy
 
 
-def gather_kernel(features_ref, aux_ref, frows_ref, fcols_ref, arows_ref, acols_ref, own, fr, fc, ar, ac):
+def link(source, target, sems, k, device):
+    return pltpu.make_async_remote_copy(
+        src_ref=source, dst_ref=target, send_sem=sems.at[0, k], recv_sem=sems.at[1, k],
+        device_id=device, device_id_type=MESH,
+    )
+
+
+def spread(row, col, arrays):
+    rows_n, cols_n = lax.axis_size("row"), lax.axis_size("col")
+    chips = rows_n // 2
+    chip, core = row // 2, lax.rem(row, 2)
+    twin = (2 * chip + 1 - core, col)
+
+    def inside(at):
+        return (at >= 0) & (at < cols_n)
+
+    def relay(array, t, step):
+        source, by_col, _, sems = array
+        slot = col - step * t
+        return link(source if t == 0 else by_col.at[slot], by_col.at[slot],
+                    sems[0] if step == 1 else sems[1], t, (row, col + step))
+
+    def sends(t, step, act):
+        @pl.when(inside(col - step * t) & inside(col + step))
+        def _():
+            for array in arrays:
+                act(relay(array, t, step))
+
+    def arrival(t, step):
+        @pl.when(inside(col - step * (t + 1)))
+        def _():
+            for _, by_col, _, sems in arrays:
+                slot = by_col.at[col - step * (t + 1)]
+                link(slot, slot, sems[0] if step == 1 else sems[1], t, (row, col - step)).wait_recv()
+
+    def cross(array, k):
+        source, _, by_row, sems = array
+        return link(source, by_row.at[row], sems[2], k, (2 * lax.rem(chip + k, chips) + core, col))
+
+    def pass_on(array, k):
+        source, _, by_row, sems = array
+        slot = 2 * lax.rem(chip + chips - k, chips) + core
+        return link(source if k == 0 else by_row.at[slot], by_row.at[slot], sems[3], k, twin)
+
+    def forward(k):
+        for array in arrays:
+            cross(array, k).wait_recv()
+            pass_on(array, k).start()
+
+    for step in (1, -1):
+        sends(0, step, lambda copy: copy.start())
+    for k in range(1, chips):
+        for array in arrays:
+            cross(array, k).start()
+    for array in arrays:
+        pass_on(array, 0).start()
+    for t in range(cols_n - 1):
+        for step in (1, -1):
+            arrival(t, step)
+            if t + 1 < cols_n - 1:
+                sends(t + 1, step, lambda copy: copy.start())
+        if t + 1 < chips:
+            forward(t + 1)
+    for k in range(cols_n, chips):
+        forward(k)
+    for t in range(cols_n - 1):
+        for step in (1, -1):
+            sends(t, step, lambda copy: copy.wait_send())
+    for array in arrays:
+        for k in range(1, chips):
+            cross(array, k).wait_send()
+        for k in range(chips):
+            pass_on(array, k).wait()
+
+
+def gather_kernel(features_ref, aux_ref, frows_ref, fcols_ref, arows_ref, acols_ref, own, *sems):
     row, col, along_row, along_col = peers()
     local = []
     for at, (src, dst, place) in enumerate((
@@ -73,16 +148,8 @@
         local.append(pltpu.make_async_copy(src, dst.at[place], own.at[at]))
         local[-1].start()
     greet(along_row, along_col)
-    copies = []
-    for k, device in along_col:
-        copies.append(send(features_ref, frows_ref.at[col], fr, k, device))
-    for k, device in along_row:
-        copies.append(send(features_ref, fcols_ref.at[row], fc, k, device))
-    for k, device in along_col:
-        copies.append(send(aux_ref, arows_ref.at[col], ar, k, device))
-    for k, device in along_row:
-        copies.append(send(aux_ref, acols_ref.at[row], ac, k, device))
-    for copy in local + copies:
+    spread(row, col, [(features_ref, frows_ref, fcols_ref, sems[:4]), (aux_ref, arows_ref, acols_ref, sems[4:])])
+    for copy in local:
         copy.wait()
 
 
@@ -99,21 +166,15 @@
     return total / molecules
 
 
-def turn_kernel(molecules, dim, pull_ref, arows_ref, acols_ref, inbox, mine, rs, ar, ac):
+def turn_kernel(molecules, dim, pull_ref, arows_ref, acols_ref, inbox, mine, rs, *sems):
     row, col, along_row, along_col = peers()
     greet(along_row, along_col)
     total = reduce_shares(pull_ref, inbox, rs, col, along_col, molecules)
     aux = with_norms(total[:, :dim], 0.0)
     mine[...] = aux
-    copies = []
-    for k, device in along_col:
-        copies.append(send(mine, arows_ref.at[col], ar, k, device))
-    for k, device in along_row:
-        copies.append(send(mine, acols_ref.at[row], ac, k, device))
     arows_ref[col] = aux
     acols_ref[row] = aux
-    for copy in copies:
-        copy.wait()
+    spread(row, col, [(mine, arows_ref, acols_ref, sems)])
 
 
 def last_kernel(molecules, pull_ref, part_ref, share_ref, total_ref, inbox, rowbox, colbox, mine, rs, sr, sc):
@@ -214,6 +275,7 @@
     any_spec = pl.BlockSpec(memory_space=pl.ANY)
     vmem = pl.BlockSpec(memory_space=pltpu.VMEM)
     dma = pltpu.SemaphoreType.DMA
+    spread_sems = [dma((2, cols_n))] * 2 + [dma((2, rows_n // 2))] * 2
 
     def shape(*sizes, dtype=f32):
         return jax.ShapeDtypeStruct(sizes, dtype)
@@ -233,7 +295,7 @@
             shape(cols_n, share_len, LANES),
             shape(rows_n, share_len, LANES),
         ],
-        scratch_shapes=[dma((4,)), dma((2, cols_n)), dma((2, rows_n)), dma((2, cols_n)), dma((2, rows_n))],
+        scratch_shapes=[dma((4,))] + spread_sems + spread_sems,
         compiler_params=comm(0),
     )(features, aux)
 
@@ -272,7 +334,7 @@
             in_specs=[vmem],
             out_specs=[vmem, vmem],
             out_shape=[shape(cols_n, share_len, LANES), shape(rows_n, share_len, LANES)],
-            scratch_shapes=[inbox, mine, dma((2, cols_n)), dma((2, cols_n)), dma((2, rows_n))],
+            scratch_shapes=[inbox, mine, dma((2, cols_n))] + spread_sems,
             compiler_params=comm(sweep),
         )(pull.reshape(cols_n, share_len, LANES))
         pull, misfits = tiles(False, dissim, arows.reshape(row_len, LANES), acols.reshape(col_len, LANES))

time: 296 us -> 270 us (0.912)
  Pallas kernels: 282 us -> 256 us
    pallas_call x1, Pallas kernels: 118 us -> 92.4 us  [on_device(): pl.pallas_call(gather_kernel, in_specs=[any_spec, any_spec], out_specs=[a...]
where the time goes in v3:
time: 270 us
  Pallas kernels  256 us (95%)
  other arithmetic  5.63 us (2%)
  local copies, waits for them, and re-layouts  5.12 us (2%)
  between operations  3.16 us (1%)
    pallas_call x1, Pallas kernels, on_device(): pl.pallas_call(gather_kernel, in_specs=[any_spec, any_spec], out_specs=[a...  92.4 us
    pallas_call x2, Pallas kernels, tiles(): pl.pallas_call(functools.partial(tile_kernel, first, chunk, dim), grid=(s...  78.3 us
    pallas_call x1, Pallas kernels, on_device(): pl.pallas_call(functools.partial(turn_kernel, molecules, dim), in_specs=[...  51.4 us
    pallas_call x1, Pallas kernels, on_device(): pl.pallas_call(functools.partial(last_kernel, molecules), in_specs=[vmem,...  33.9 us

profile of v3, /device:TPU:8, one launch (start us, length us, event | category | flops | bytes accessed | tf_op | source)
XLA Modules:
  0.0 270.0 jit_solution(5490714978870502206)
XLA Ops:
  0.6 1.5 multiply_reduce_fusion
  2.1 1.0 copy.7
  3.2 0.2 fusion.2
  3.3 0.2 select_select_fusion
  3.5 0.8 pad_maximum_fusion.aux_ref
  4.4 92.4 %shard_map.49 = (bf16[4,512,1024]{2,1,0:T(8,128)(2,1)}, bf16[8,512,1024]{2,1,0:T(8,128)(2,1)}, f32[4,512,128]{2,1,0:T(8,128)}, f32[8,512,128]{2,1,0:T(8,128)}) custom-call(bf16[512,1024]{1,0:T(8,128)(2,1)} %features_ref.1, f32[512,128]{1,0:T(8,128)} %pad_maximum_fusion.aux_ref), custom_call_target="tpu_custom_call" | custom-call | tf_op jit(solution)/shard_map/pallas_call | solution.py:288
  96.8 46.4 %shard_map.50 = (f32[2048,4096]{1,0:T(8,128)}, f32[2048,128]{1,0:T(8,128)}, f32[8,8,128]{2,1,0:T(8,128)}) custom-call(bf16[2048,1024]{1,0:T(8,128)(2,1)} %bitcast.16, bf16[4096,1024]{1,0:T(8,128)(2,1)} %bitcast.15, f32[2048,128]{1,0:T(8,128)} %bitcast.23, f32[4096,128]{1,0:T(8,128)} %bitcast.18), custom_call_target="tpu_custom_call" | custom-call | tf_op jit(solution)/shard_map/pallas_call | solution.py:311
  143.2 0.8 reduce_sum.48
  143.9 51.4 %shard_map.51 = (f32[4,512,128]{2,1,0:T(8,128)}, f32[8,512,128]{2,1,0:T(8,128)}) custom-call(f32[4,512,128]{2,1,0:T(8,128)} %bitcast.22), custom_call_target="tpu_custom_call" | custom-call | tf_op jit(solution)/shard_map/pallas_call | solution.py:332
  195.4 32.0 %shard_map.52 = (f32[2048,128]{1,0:T(8,128)}, f32[8,8,128]{2,1,0:T(8,128)}) custom-call(f32[2048,4096]{1,0:T(8,128)} %get-tuple-element.20.refs_0_, f32[2048,128]{1,0:T(8,128)} %bitcast.20, f32[4096,128]{1,0:T(8,128)} %bitcast.19), custom_call_target="tpu_custom_call" | custom-call | tf_op jit(solution)/shard_map/pallas_call | solution.py:311
  227.3 0.8 reduce_sum.47
  228.1 0.6 pad_maximum_fusion.1.part_ref
  228.7 33.9 %shard_map.53 = (f32[512,128]{1,0:T(8,128)}, f32[2,8,128]{2,1,0:T(8,128)}) custom-call(f32[4,512,128]{2,1,0:T(8,128)} %bitcast.21, f32[2,8,128]{2,1,0:T(8,128)} %pad_maximum_fusion.1.part_ref), custom_call_target="tpu_custom_call" | custom-call | tf_op jit(solution)/shard_map/pallas_call | solution.py:342
  262.6 0.8 reduce_sum.49
  263.4 0.6 fusion.3
  265.3 1.8 slice_reduce_fusion
  267.1 1.0 slice_bitcast_fusion
  268.1 0.8 copy.8
  (1 shorter events, 0.0 us)

commit v4 on v3

--- a/solution.py
+++ b/solution.py
@@ -154,10 +154,12 @@
 
 
 def reduce_shares(pull_ref, inbox, sems, col, along_col, molecules):
+    length = inbox.shape[2]
+    share_of = lambda at: pl.ds(pl.multiple_of(at * length, LANES), length)
     copies = []
     for k, device in along_col:
-        copies.append(send(pull_ref.at[device[1]], inbox.at[col], sems, k, device))
-    inbox[col] = pull_ref[col]
+        copies.append(send(pull_ref.at[:, share_of(device[1])], inbox.at[col], sems, k, device))
+    inbox[col] = pull_ref[:, share_of(col)]
     for copy in copies:
         copy.wait()
     total = inbox[0]
@@ -166,15 +168,19 @@
     return total / molecules
 
 
-def turn_kernel(molecules, dim, pull_ref, arows_ref, acols_ref, inbox, mine, rs, *sems):
+def turn_kernel(molecules, dim, pull_ref, arows_ref, acols_ref, inbox, rowsbox, colsbox, mine, rs, *sems):
     row, col, along_row, along_col = peers()
     greet(along_row, along_col)
     total = reduce_shares(pull_ref, inbox, rs, col, along_col, molecules)
-    aux = with_norms(total[:, :dim], 0.0)
-    mine[...] = aux
-    arows_ref[col] = aux
-    acols_ref[row] = aux
-    spread(row, col, [(mine, arows_ref, acols_ref, sems)])
+    used, length = mine.shape
+    mine[...] = with_norms(total[:dim].T, 0.0).T[:used]
+    rowsbox[col] = mine[...]
+    colsbox[row] = mine[...]
+    spread(row, col, [(mine, rowsbox, colsbox, sems)])
+    pad = jnp.zeros((LANES - used, length), jnp.float32)
+    for box, out in ((rowsbox, arows_ref), (colsbox, acols_ref)):
+        for at in range(box.shape[0]):
+            out[at] = jnp.concatenate([box[at], pad], axis=0).T
 
 
 def last_kernel(molecules, pull_ref, part_ref, share_ref, total_ref, inbox, rowbox, colbox, mine, rs, sr, sc):
@@ -255,7 +261,8 @@
         moved += jnp.dot(rest, weights[at, :], preferred_element_type=jnp.float32)
     pull = x * moved[:, 2 * dim : 2 * dim + 1] - (moved[:, :dim] + moved[:, dim : 2 * dim])
     stress = jnp.sum(squares, axis=1, keepdims=True)
-    pull_ref[...] = jnp.concatenate([pull, jnp.broadcast_to(stress, (tile, LANES - dim))], axis=1)
+    packed = jnp.concatenate([pull, jnp.broadcast_to(stress, (tile, LANES - dim))], axis=1)
+    pull_ref[...] = packed.T[: pull_ref.shape[0]]
     square_ref[...] = rows_sum(squares)[None]
 
 
@@ -270,6 +277,7 @@
     tile = 256
     chunk = 512
     steps = row_len // tile
+    used = dim + 8
     big = 56 * 1024 * 1024
     f32 = jnp.float32
     any_spec = pl.BlockSpec(memory_space=pl.ANY)
@@ -304,8 +312,8 @@
 
     def tiles(first, *given):
         specs = [by_row(feat), whole(col_len, feat)] if first else [by_row(col_len)]
-        outs = [by_row(LANES), pl.BlockSpec((1, 8, LANES), lambda i: (i, 0, 0))]
-        shapes = [shape(row_len, LANES), shape(steps, 8, LANES)]
+        outs = [pl.BlockSpec((used, tile), lambda i: (0, i)), pl.BlockSpec((1, 8, LANES), lambda i: (i, 0, 0))]
+        shapes = [shape(used, row_len), shape(steps, 8, LANES)]
         if first:
             outs, shapes = [by_row(col_len)] + outs, [shape(row_len, col_len)] + shapes
         return pl.pallas_call(
@@ -326,32 +334,32 @@
         True, frows.reshape(row_len, feat), fcols.reshape(col_len, feat),
         arows.reshape(row_len, LANES), acols.reshape(col_len, LANES),
     )
-    inbox = pltpu.VMEM((cols_n, share_len, LANES), f32)
-    mine = pltpu.VMEM((share_len, LANES), f32)
+    inbox = pltpu.VMEM((cols_n, used, share_len), f32)
+    boxes = [inbox, inbox, pltpu.VMEM((rows_n, used, share_len), f32), pltpu.VMEM((used, share_len), f32)]
     for sweep in range(1, ITERS):
         arows, acols = pl.pallas_call(
             functools.partial(turn_kernel, molecules, dim),
             in_specs=[vmem],
             out_specs=[vmem, vmem],
             out_shape=[shape(cols_n, share_len, LANES), shape(rows_n, share_len, LANES)],
-            scratch_shapes=[inbox, mine, dma((2, cols_n))] + spread_sems,
+            scratch_shapes=boxes + [dma((2, cols_n))] + spread_sems,
             compiler_params=comm(sweep),
-        )(pull.reshape(cols_n, share_len, LANES))
+        )(pull)
         pull, misfits = tiles(False, dissim, arows.reshape(row_len, LANES), acols.reshape(col_len, LANES))
     parts = jnp.stack([jnp.sum(misfits, axis=0), jnp.sum(dis_squares, axis=0)])
     share, totals = pl.pallas_call(
         functools.partial(last_kernel, molecules),
         in_specs=[vmem, vmem],
         out_specs=[vmem, vmem],
-        out_shape=[shape(share_len, LANES), shape(2, 8, LANES)],
+        out_shape=[shape(used, share_len), shape(2, 8, LANES)],
         scratch_shapes=[
             inbox, pltpu.VMEM((rows_n, 2, 8, LANES), f32), pltpu.VMEM((cols_n, 2, 8, LANES), f32),
             pltpu.VMEM((2, 8, LANES), f32), dma((2, cols_n)), dma((2, rows_n)), dma((2, cols_n)),
         ],
         compiler_params=comm(ITERS),
-    )(pull.reshape(cols_n, share_len, LANES), parts)
+    )(pull, parts)
     totals = jnp.sum(totals, axis=(1, 2))
-    return (share[:, :dim].T, share[:, dim], totals[0] / totals[1])
+    return (share[:dim], share[dim], totals[0] / totals[1])
 
 
 def solution(mesh):

time: 270 us -> 246 us (0.911)
  Pallas kernels: 256 us -> 232 us
    pallas_call x1, Pallas kernels: 51.4 us -> 37.2 us  [on_device(): pl.pallas_call(functools.partial(turn_kernel, molecules, dim), in_specs=[...]
    pallas_call x1, Pallas kernels: 33.9 us -> 23.7 us  [on_device(): pl.pallas_call(functools.partial(last_kernel, molecules), in_specs=[vmem,...]
where the time goes in v4:
time: 246 us
  Pallas kernels  232 us (94%)
  other arithmetic  5.63 us (2%)
  local copies, waits for them, and re-layouts  4.48 us (2%)
  between operations  3.15 us (1%)
    pallas_call x1, Pallas kernels, on_device(): pl.pallas_call(gather_kernel, in_specs=[any_spec, any_spec], out_specs=[a...  92.4 us
    pallas_call x2, Pallas kernels, tiles(): pl.pallas_call(functools.partial(tile_kernel, first, chunk, dim), grid=(s...  79.2 us
    pallas_call x1, Pallas kernels, on_device(): pl.pallas_call(functools.partial(turn_kernel, molecules, dim), in_specs=[...  37.2 us
    pallas_call x1, Pallas kernels, on_device(): pl.pallas_call(functools.partial(last_kernel, molecules), in_specs=[vmem,...  23.7 us

profile of v4, /device:TPU:8, one launch (start us, length us, event | category | flops | bytes accessed | tf_op | source)
XLA Modules:
  0.0 245.7 jit_solution(11703363067944708473)
XLA Ops:
  0.6 1.5 multiply_reduce_fusion
  2.1 1.0 copy.5
  3.2 0.2 fusion.2
  3.3 0.2 select_select_fusion
  3.5 0.8 pad_maximum_fusion.aux_ref
  4.4 92.4 %shard_map.49 = (bf16[4,512,1024]{2,1,0:T(8,128)(2,1)}, bf16[8,512,1024]{2,1,0:T(8,128)(2,1)}, f32[4,512,128]{2,1,0:T(8,128)}, f32[8,512,128]{2,1,0:T(8,128)}) custom-call(bf16[512,1024]{1,0:T(8,128)(2,1)} %features_ref.1, f32[512,128]{1,0:T(8,128)} %pad_maximum_fusion.aux_ref), custom_call_target="tpu_custom_call" | custom-call | tf_op jit(solution)/shard_map/pallas_call | solution.py:296
  96.8 46.7 %shard_map.50 = (f32[2048,4096]{1,0:T(8,128)}, f32[72,2048]{1,0:T(8,128)}, f32[8,8,128]{2,1,0:T(8,128)}) custom-call(bf16[2048,1024]{1,0:T(8,128)(2,1)} %bitcast.13, bf16[4096,1024]{1,0:T(8,128)(2,1)} %bitcast.12, f32[2048,128]{1,0:T(8,128)} %bitcast.18, f32[4096,128]{1,0:T(8,128)} %bitcast.15), custom_call_target="tpu_custom_call" | custom-call | tf_op jit(solution)/shard_map/pallas_call | solution.py:319
  143.5 0.8 reduce_sum.48
  144.2 37.2 %shard_map.51 = (f32[4,512,128]{2,1,0:T(8,128)}, f32[8,512,128]{2,1,0:T(8,128)}) custom-call(f32[72,2048]{1,0:T(8,128)} %get-tuple-element.21.pull_ref), custom_call_target="tpu_custom_call" | custom-call | tf_op jit(solution)/shard_map/pallas_call | solution.py:340
  181.4 32.5 %shard_map.52 = (f32[72,2048]{1,0:T(8,128)}, f32[8,8,128]{2,1,0:T(8,128)}) custom-call(f32[2048,4096]{1,0:T(8,128)} %get-tuple-element.20.refs_0_, f32[2048,128]{1,0:T(8,128)} %bitcast.17, f32[4096,128]{1,0:T(8,128)} %bitcast.16), custom_call_target="tpu_custom_call" | custom-call | tf_op jit(solution)/shard_map/pallas_call | solution.py:319
  213.9 0.8 reduce_sum.47
  214.7 0.6 pad_maximum_fusion.1.part_ref
  215.3 23.7 %shard_map.53 = (f32[72,512]{1,0:T(8,128)}, f32[2,8,128]{2,1,0:T(8,128)}) custom-call(f32[72,2048]{1,0:T(8,128)} %get-tuple-element.24.pull_ref, f32[2,8,128]{2,1,0:T(8,128)} %pad_maximum_fusion.1.part_ref), custom_call_target="tpu_custom_call" | custom-call | tf_op jit(solution)/shard_map/pallas_call | solution.py:350
  239.0 0.8 reduce_sum.49
  239.8 0.6 fusion.3
  241.7 1.3 slice.13
  243.0 1.6 slice.12
  (1 shorter events, 0.0 us)

commit v5 on v4

--- a/solution.py
+++ b/solution.py
@@ -153,17 +153,21 @@
         copy.wait()
 
 
-def reduce_shares(pull_ref, inbox, sems, col, along_col, molecules):
+def start_shares(pull_ref, inbox, sems, col, along_col):
     length = inbox.shape[2]
     share_of = lambda at: pl.ds(pl.multiple_of(at * length, LANES), length)
     copies = []
     for k, device in along_col:
         copies.append(send(pull_ref.at[:, share_of(device[1])], inbox.at[col], sems, k, device))
     inbox[col] = pull_ref[:, share_of(col)]
+    return copies
+
+
+def finish_shares(copies, inbox, molecules):
     for copy in copies:
         copy.wait()
     total = inbox[0]
-    for at in range(1, len(along_col) + 1):
+    for at in range(1, inbox.shape[0]):
         total += inbox[at]
     return total / molecules
 
@@ -171,7 +175,7 @@
 def turn_kernel(molecules, dim, pull_ref, arows_ref, acols_ref, inbox, rowsbox, colsbox, mine, rs, *sems):
     row, col, along_row, along_col = peers()
     greet(along_row, along_col)
-    total = reduce_shares(pull_ref, inbox, rs, col, along_col, molecules)
+    total = finish_shares(start_shares(pull_ref, inbox, rs, col, along_col), inbox, molecules)
     used, length = mine.shape
     mine[...] = with_norms(total[:dim].T, 0.0).T[:used]
     rowsbox[col] = mine[...]
@@ -190,6 +194,7 @@
     for k, device in along_row:
         copies.append(send(part_ref, rowbox.at[row], sr, k, device))
     rowbox[row] = part_ref[...]
+    shares = start_shares(pull_ref, inbox, rs, col, along_col)
     for copy in copies:
         copy.wait()
     total = rowbox[0]
@@ -200,7 +205,7 @@
     for k, device in along_col:
         copies.append(send(mine, colbox.at[col], sc, k, device))
     colbox[col] = total
-    share_ref[...] = reduce_shares(pull_ref, inbox, rs, col, along_col, molecules)
+    share_ref[...] = finish_shares(shares, inbox, molecules)
     for copy in copies:
         copy.wait()
     total = colbox[0]

time: 246 us -> 246 us (level)
  no operation moved by 1% of the time
where the time goes in v5:
time: 246 us; the launch traced here: 243 us
  Pallas kernels  230 us (93%)
  other arithmetic  5.63 us (2%)
  local copies, waits for them, and re-layouts  4.48 us (2%)
  between operations  3.15 us (1%)
    pallas_call x1, Pallas kernels, on_device(): pl.pallas_call(gather_kernel, in_specs=[any_spec, any_spec], out_specs=[a...  92.4 us
    pallas_call x2, Pallas kernels, tiles(): pl.pallas_call(functools.partial(tile_kernel, first, chunk, dim), grid=(s...  79.2 us
    pallas_call x1, Pallas kernels, on_device(): pl.pallas_call(functools.partial(turn_kernel, molecules, dim), in_specs=[...  37.2 us
    pallas_call x1, Pallas kernels, on_device(): pl.pallas_call(functools.partial(last_kernel, molecules), in_specs=[vmem,...  21.3 us

profile of v5, /device:TPU:8, one launch (start us, length us, event | category | flops | bytes accessed | tf_op | source)
XLA Modules:
  0.0 243.3 jit_solution(8622316109067112391)
XLA Ops:
  0.6 1.5 multiply_reduce_fusion
  2.1 1.0 copy.5
  3.2 0.2 fusion.2
  3.3 0.2 select_select_fusion
  3.5 0.8 pad_maximum_fusion.aux_ref
  4.4 92.4 %shard_map.49 = (bf16[4,512,1024]{2,1,0:T(8,128)(2,1)}, bf16[8,512,1024]{2,1,0:T(8,128)(2,1)}, f32[4,512,128]{2,1,0:T(8,128)}, f32[8,512,128]{2,1,0:T(8,128)}) custom-call(bf16[512,1024]{1,0:T(8,128)(2,1)} %features_ref.1, f32[512,128]{1,0:T(8,128)} %pad_maximum_fusion.aux_ref), custom_call_target="tpu_custom_call" | custom-call | tf_op jit(solution)/shard_map/pallas_call | solution.py:301
  96.8 46.7 %shard_map.50 = (f32[2048,4096]{1,0:T(8,128)}, f32[72,2048]{1,0:T(8,128)}, f32[8,8,128]{2,1,0:T(8,128)}) custom-call(bf16[2048,1024]{1,0:T(8,128)(2,1)} %bitcast.13, bf16[4096,1024]{1,0:T(8,128)(2,1)} %bitcast.12, f32[2048,128]{1,0:T(8,128)} %bitcast.18, f32[4096,128]{1,0:T(8,128)} %bitcast.15), custom_call_target="tpu_custom_call" | custom-call | tf_op jit(solution)/shard_map/pallas_call | solution.py:324
  143.5 0.8 reduce_sum.48
  144.2 37.2 %shard_map.51 = (f32[4,512,128]{2,1,0:T(8,128)}, f32[8,512,128]{2,1,0:T(8,128)}) custom-call(f32[72,2048]{1,0:T(8,128)} %get-tuple-element.21.pull_ref), custom_call_target="tpu_custom_call" | custom-call | tf_op jit(solution)/shard_map/pallas_call | solution.py:345
  181.4 32.5 %shard_map.52 = (f32[72,2048]{1,0:T(8,128)}, f32[8,8,128]{2,1,0:T(8,128)}) custom-call(f32[2048,4096]{1,0:T(8,128)} %get-tuple-element.20.refs_0_, f32[2048,128]{1,0:T(8,128)} %bitcast.17, f32[4096,128]{1,0:T(8,128)} %bitcast.16), custom_call_target="tpu_custom_call" | custom-call | tf_op jit(solution)/shard_map/pallas_call | solution.py:324
  213.9 0.8 reduce_sum.47
  214.7 0.6 pad_maximum_fusion.1.part_ref
  215.3 21.3 %shard_map.53 = (f32[72,512]{1,0:T(8,128)}, f32[2,8,128]{2,1,0:T(8,128)}) custom-call(f32[72,2048]{1,0:T(8,128)} %get-tuple-element.24.pull_ref, f32[2,8,128]{2,1,0:T(8,128)} %pad_maximum_fusion.1.part_ref), custom_call_target="tpu_custom_call" | custom-call | tf_op jit(solution)/shard_map/pallas_call | solution.py:355
  236.5 0.8 reduce_sum.49
  237.3 0.6 fusion.3
  239.3 1.3 slice.13
  240.6 1.6 slice.12
  (1 shorter events, 0.0 us)
